TPU v7x, 512 devices: a whole 4x8x8 slice. The times are simulated.
512 devices in a mesh: group: 16 (over y, x_lo), fsdp: 32 (over x_hi, z, core).
Axes of the slice: x: 4 (x_hi: 2, x_lo: 2; x = x_hi * 2 + x_lo), y: 8, z: 8, core: 2. Of those that a mesh axis runs over, the one named last changes fastest.
Arguments:
- grad_terms: bfloat16 [16, 32, 64, 8192], P('group', 'fsdp'), may hold values from -0.59765625 to 0.59765625
- master: float32 [64, 8192], P('fsdp'), may hold values from -6 to 6
- inner_drift: float32 [16, 64, 8192], P('group', 'fsdp'), may hold values from -0.6 to 0.6
- momentum: float32 [64, 8192], P('fsdp'), may hold values from -3 to 3
- moment_codes: int32 [16, 64, 8192], P('group', 'fsdp'), may hold values from 0 to 255
- second_codes: int32 [16, 64, 8192], P('group', 'fsdp'), may hold values from 0 to 255
- moment_scale: float32 [16, 64, 32], P('group', 'fsdp'), may hold values from 0.01 to 0.1
- second_scale: float32 [16, 64, 32], P('group', 'fsdp'), may hold values from 0.05 to 0.5
- counts: int32 [16], P('group'), may hold values from 256 to 6144, as said below
Outputs:
- master_new: float32 [64, 8192], P('fsdp')
- momentum_new: float32 [64, 8192], P('fsdp')
- moment_new: float32 [16, 64, 8192], P('group', 'fsdp')
- second_new: float32 [16, 64, 8192], P('group', 'fsdp')
- model_copy: bfloat16 [64, 8192], replicated
Inputs may be any that keep to these rules, and one draw needn't show every extreme that they name: `counts`: one group trained on 6144 tokens, every other on 256 to 2048.
All inputs are finite; a program needn't handle non-finite values.
Results may differ from a plain program's by a relative error of at most 0.0004.
Values may be sent and summed in bfloat16 or wider, within the bound.
A program may use at most 64 MiB of HBM per device.

v0:
```python
import jax
import jax.numpy as jnp
from jax import lax
from jax.sharding import PartitionSpec as P

BLOCK = 256
STEP = 500


def blockwise(values, scale):
    shaped = values.reshape(values.shape[:-1] + (values.shape[-1] // BLOCK, BLOCK))
    return (shaped * scale[..., None]).reshape(values.shape)


def nesterov(mean_pseudo, master, momentum):
    momentum_new = 0.9 * momentum + mean_pseudo
    master_new = master - 0.7 * (mean_pseudo + 0.9 * momentum_new)
    return (master_new, momentum_new)


def on_device(
    grad_terms,
    master,
    inner_drift,
    momentum,
    moment_codes,
    second_codes,
    moment_scale,
    second_scale,
    counts,
):
    inner = master + inner_drift[0]
    weight = counts.astype(jnp.float32)[0]
    summed = lax.psum_scatter(
        grad_terms.astype(jnp.float32), "fsdp", scatter_dimension=2, tiled=True
    )
    grad = summed[:, 0]
    signed = (moment_codes.astype(jnp.float32) - 127.5) / 127.5
    moment_old = blockwise(signed * signed * signed, moment_scale)
    unsigned = (second_codes.astype(jnp.float32) + 16.0) / 271.0
    second_old = blockwise(unsigned * unsigned, second_scale)
    moment_new = 0.9 * moment_old + 0.1 * grad
    second_new = 0.999 * second_old + 0.001 * grad * grad
    update = moment_new / (1.0 - 0.9**STEP) / (jnp.sqrt(second_new / (1.0 - 0.999**STEP)) + 1e-08)
    pseudo = master - (inner - 0.8 * (update[0] + 0.025 * inner))
    weighted = weight * pseudo
    total_rows, total_count = lax.psum((weighted, weight), "group")
    master_new, momentum_new = nesterov(total_rows / total_count, master, momentum)
    model_copy = lax.all_gather(master_new.astype(jnp.bfloat16), "fsdp", axis=0, tiled=True)
    return (master_new, momentum_new, moment_new, second_new, model_copy)


def solution(mesh):
    in_specs = (
        P("group", "fsdp", None, None),
        P("fsdp", None),
        P("group", "fsdp", None),
        P("fsdp", None),
        P("group", "fsdp", None),
        P("group", "fsdp", None),
        P("group", "fsdp", None),
        P("group", "fsdp", None),
        P("group"),
    )
    out_specs = (
        P("fsdp", None),
        P("fsdp", None),
        P("group", "fsdp", None),
        P("group", "fsdp", None),
        P(),
    )
    return jax.shard_map(
        on_device, mesh=mesh, in_specs=in_specs, out_specs=out_specs, check_vma=False
    )
```

profile of v0, /device:TPU:1, one launch (start us, length us, event | category | flops | bytes accessed | tf_op | source)
XLA Modules:
  0.0 398.8 jit_solution(11685884509597873997)
XLA Ops:
  7.2 0.0 copy-start.5
  7.2 0.0 copy-start.6
  7.2 0.0 copy-start
  7.2 0.0 copy-start.1
  7.2 0.0 copy-start.3
  7.2 0.0 copy-start.2
  7.2 0.0 all-reduce.4.cloned.1.call-start
  8.0 0.0 copy-start.4
  8.0 157.2 %all-reduce.5 = f32[1,1,64,8192]{3,2,1,0:T(8,128)S(1)} all-reduce(bf16[1,1,64,8192]{3,2,1,0:T(8,128)(2,1)} %param.9), channel_id=2, replica_groups=mesh['group'=16,'fsdp'=32] {'fsdp'}, use_global_device_ids=true, to_apply=%region_0.0.clone | all-reduce | flops 524288 | bytes 3145728
  165.1 0.0 copy-done.5
  165.2 0.1 mul.137
  165.3 0.0 copy-done.6
  165.3 0.1 mul.146
  165.4 1.3 dynamic-slice
  167.3 0.0 copy-done
  167.4 0.0 copy-done.1
  167.4 0.0 copy-done.3
  167.4 0.0 copy-done.2
  167.4 1.0 fusion.7
  168.4 0.0 all-reduce.4.cloned.1.call-update
  168.4 0.0 all-gather.3.cloned.1.call-start
  168.5 28.3 %psum.15 = f32[]{:T(128)} all-reduce(f32[]{:T(128)} %bitcast.2), channel_id=1, replica_groups=mesh['group'=16,'fsdp'=32] {'group'}, use_global_device_ids=true, to_apply=%region_2.0 | all-reduce | flops 1 | bytes 8 | tf_op jit(solution)/shard_map/psum | solution.py:47
  196.8 95.9 %all-reduce.4.cloned.1.call-done = f32[2,8192]{1,0:T(2,128)} async-done(((f32[2,8192]{1,0:T(2,128)}), f32[2,8192]{1,0:T(2,128)}) %all-reduce.4.cloned.1.call-update) | async-done | bytes 65552 | tf_op jit(solution)/shard_map/psum | solution.py:47
  292.7 0.0 copy-done.4
  292.7 2.2 convert_bitcast_fusion
  294.9 0.0 all-gather.3.cloned.1.call-update
  295.0 94.7 %all-gather.3.cloned.1.call-done = bf16[32,2,8192]{2,1,0:T(2,128)(2,1)} async-done(((bf16[1,2,8192]{2,1,0:T(2,128)(2,1)}), bf16[32,2,8192]{2,1,0:T(2,128)(2,1)}) %all-gather.3.cloned.1.call-update) | async-done | bytes 1048592 | tf_op jit(solution)/shard_map/all_gather | solution.py:49
  389.7 2.2 reshape.84
  (2 shorter events, 0.1 us)
Async XLA Ops:
  7.2 158.0 %copy-start.5 = (f32[1,2,32]{2,1,0:T(2,128)S(1)}, f32[1,2,32]{2,1,0:T(2,128)}, u32[]{:S(2)}) copy-start(f32[1,2,32]{2,1,0:T(2,128)} %param.15) | copy-start | bytes 772
  7.2 158.1 %copy-start.6 = (f32[1,2,32]{2,1,0:T(2,128)S(1)}, f32[1,2,32]{2,1,0:T(2,128)}, u32[]{:S(2)}) copy-start(f32[1,2,32]{2,1,0:T(2,128)} %param.16) | copy-start | bytes 772
  7.2 160.2 %copy-start = (f32[2,8192]{1,0:T(2,128)S(1)}, f32[2,8192]{1,0:T(2,128)}, u32[]{:S(2)}) copy-start(f32[2,8192]{1,0:T(2,128)} %param.10) | copy-start | bytes 196612
  7.2 160.2 %copy-start.1 = (f32[1,2,8192]{2,1,0:T(2,128)S(1)}, f32[1,2,8192]{2,1,0:T(2,128)}, u32[]{:S(2)}) copy-start(f32[1,2,8192]{2,1,0:T(2,128)} %param.11) | copy-start | bytes 196612
  7.2 160.2 %copy-start.3 = (s32[1,2,8192]{2,1,0:T(2,128)S(1)}, s32[1,2,8192]{2,1,0:T(2,128)}, u32[]{:S(2)}) copy-start(s32[1,2,8192]{2,1,0:T(2,128)} %param.13) | copy-start | bytes 196612
  7.2 160.2 %copy-start.2 = (s32[1,2,8192]{2,1,0:T(2,128)S(1)}, s32[1,2,8192]{2,1,0:T(2,128)}, u32[]{:S(2)}) copy-start(s32[1,2,8192]{2,1,0:T(2,128)} %param.14) | copy-start | bytes 196612
  7.2 285.5 %all-reduce.4.cloned.1.call-start = ((), (), s32[]{:S(2)}) async-start(), calls=%async_computation | async-start | bytes 131072 | tf_op jit(solution)/shard_map/psum | solution.py:47
  8.0 284.7 %copy-start.4 = (f32[2,8192]{1,0:T(2,128)S(1)}, f32[2,8192]{1,0:T(2,128)}, u32[]{:S(2)}) copy-start(f32[2,8192]{1,0:T(2,128)} %param.12) | copy-start | bytes 196612
  168.4 221.3 %all-gather.3.cloned.1.call-start = ((), (), s32[]{:S(2)}) async-start(), calls=%async_computation.1 | async-start | bytes 1081344 | tf_op jit(solution)/shard_map/all_gather | solution.py:49
Sparse Core Ops, SparseCore 0:
  168.5 124.1 all-reduce.3
  297.2 92.4 all-gather.2
where the time goes:
time: 399 us
  waiting for transfers between devices  191 us (48%)
  blocking collectives  185 us (46%)
  between operations  15.5 us (4%)
    unnamed x1, blocking collectives  157 us
    psum x1, waiting for transfers between devices, on_device(): total_rows, total_count = lax.psum((weighted, weight), 'group')  95.9 us
    all_gather x1, waiting for transfers between devices, on_device(): lax.all_gather(master_new.astype(jnp.bfloat16), 'fsdp', axis=0, tiled=True)  94.7 us
    psum x1, blocking collectives, on_device(): total_rows, total_count = lax.psum((weighted, weight), 'group')  28.3 us
  transfers between devices with their start and end apart: 2, of which 2 were waited for; matrix products, arithmetic and copies ran while one was open for 0% of the time, Pallas kernels for 0%

commit v1 on v0

--- a/solution.py
+++ b/solution.py
@@ -46,7 +46,12 @@
     weighted = weight * pseudo
     total_rows, total_count = lax.psum((weighted, weight), "group")
     master_new, momentum_new = nesterov(total_rows / total_count, master, momentum)
-    model_copy = lax.all_gather(master_new.astype(jnp.bfloat16), "fsdp", axis=0, tiled=True)
+    model_copy = jnp.concatenate(
+        lax.all_to_all(
+            jnp.stack([master_new.astype(jnp.bfloat16)] * lax.axis_size("fsdp")), "fsdp", 0, 0
+        ),
+        axis=0,
+    )
     return (master_new, momentum_new, moment_new, second_new, model_copy)
 
 

time: 399 us -> 354 us (0.89)
  waiting for transfers between devices: 191 us -> 96 us
  blocking collectives: 185 us -> 234 us
    all_gather x1 -> x0, waiting for transfers between devices: 94.7 us -> none  [on_device(): lax.all_gather(master_new.astype(jnp.bfloat16), 'fsdp', axis=0, tiled=True)]
    all_to_all x0 -> x1, blocking collectives: none -> 48.5 us  [on_device(): lax.all_to_all(jnp.stack([master_new.astype(jnp.bfloat16)] * lax.axis_siz...]
  transfers between devices with their start and end apart: 2 -> 1, of which waited for: 2 -> 1; matrix products, arithmetic and copies ran while one was open for 0% -> 0% of each run, Pallas kernels for 0% -> 0%
where the time goes in v1:
time: 354 us; the launch traced here: 352 us
  blocking collectives  234 us (66%)
  waiting for transfers between devices  96 us (27%)
  between operations  15.5 us (4%)
  local copies, waits for them, and re-layouts  3.66 us (1%)
    unnamed x1, blocking collectives  157 us
    psum x1, waiting for transfers between devices, on_device(): total_rows, total_count = lax.psum((weighted, weight), 'group')  96 us
    all_to_all x1, blocking collectives, on_device(): lax.all_to_all(jnp.stack([master_new.astype(jnp.bfloat16)] * lax.axis_siz...  48.5 us
    psum x1, blocking collectives, on_device(): total_rows, total_count = lax.psum((weighted, weight), 'group')  28.3 us
  transfers between devices with their start and end apart: 1, of which 1 were waited for; matrix products, arithmetic and copies ran while one was open for 0% of the time, Pallas kernels for 0%

profile of v1, /device:TPU:1, one launch (start us, length us, event | category | flops | bytes accessed | tf_op | source)
XLA Modules:
  0.0 352.4 jit_solution(10713294034037916916)
XLA Ops:
  7.2 0.0 copy-start.5
  7.2 0.0 copy-start.6
  7.2 0.0 copy-start
  7.2 0.0 copy-start.1
  7.2 0.0 copy-start.3
  7.2 0.0 copy-start.2
  7.2 0.0 all-reduce.4.cloned.1.call-start
  8.0 0.0 copy-start.4
  8.0 157.2 %all-reduce.5 = f32[1,1,64,8192]{3,2,1,0:T(8,128)S(1)} all-reduce(bf16[1,1,64,8192]{3,2,1,0:T(8,128)(2,1)} %param.9), channel_id=2, replica_groups=mesh['group'=16,'fsdp'=32] {'fsdp'}, use_global_device_ids=true, to_apply=%region_0.0.clone | all-reduce | flops 524288 | bytes 3145728
  165.1 0.0 copy-done.5
  165.2 0.1 mul.137
  165.3 0.0 copy-done.6
  165.3 0.1 mul.146
  165.4 1.3 dynamic-slice
  167.3 0.0 copy-done
  167.4 0.0 copy-done.1
  167.4 0.0 copy-done.3
  167.4 0.0 copy-done.2
  167.4 1.0 fusion.7
  168.4 0.0 all-reduce.4.cloned.1.call-update
  168.4 28.3 %psum.15 = f32[]{:T(128)} all-reduce(f32[]{:T(128)} %bitcast.2), channel_id=1, replica_groups=mesh['group'=16,'fsdp'=32] {'group'}, use_global_device_ids=true, to_apply=%region_2.0 | all-reduce | flops 1 | bytes 8 | tf_op jit(solution)/shard_map/psum | solution.py:47
  196.7 96.0 %all-reduce.4.cloned.1.call-done = f32[2,8192]{1,0:T(2,128)} async-done(((f32[2,8192]{1,0:T(2,128)}), f32[2,8192]{1,0:T(2,128)}) %all-reduce.4.cloned.1.call-update) | async-done | bytes 65552 | tf_op jit(solution)/shard_map/psum | solution.py:47
  292.7 0.0 copy-done.4
  292.7 2.2 fusion.8
  295.0 0.9 stack.2
  295.9 48.5 %all_to_all.5 = bf16[32,2,8192]{2,1,0:T(2,128)(2,1)S(1)} all-to-all(bf16[32,2,8192]{2,1,0:T(2,128)(2,1)S(1)} %stack.2), channel_id=1, replica_groups=mesh['group'=16,'fsdp'=32] {'fsdp'}, dimensions={0} | all-to-all | bytes 2097152 | tf_op jit(solution)/shard_map/all_to_all | solution.py:50
  344.4 1.2 reshape.88
  (2 shorter events, 0.1 us)
Async XLA Ops:
  7.2 158.0 %copy-start.5 = (f32[1,2,32]{2,1,0:T(2,128)S(1)}, f32[1,2,32]{2,1,0:T(2,128)}, u32[]{:S(2)}) copy-start(f32[1,2,32]{2,1,0:T(2,128)} %param.15) | copy-start | bytes 772
  7.2 158.1 %copy-start.6 = (f32[1,2,32]{2,1,0:T(2,128)S(1)}, f32[1,2,32]{2,1,0:T(2,128)}, u32[]{:S(2)}) copy-start(f32[1,2,32]{2,1,0:T(2,128)} %param.16) | copy-start | bytes 772
  7.2 160.2 %copy-start = (f32[2,8192]{1,0:T(2,128)S(1)}, f32[2,8192]{1,0:T(2,128)}, u32[]{:S(2)}) copy-start(f32[2,8192]{1,0:T(2,128)} %param.10) | copy-start | bytes 196612
  7.2 160.2 %copy-start.1 = (f32[1,2,8192]{2,1,0:T(2,128)S(1)}, f32[1,2,8192]{2,1,0:T(2,128)}, u32[]{:S(2)}) copy-start(f32[1,2,8192]{2,1,0:T(2,128)} %param.11) | copy-start | bytes 196612
  7.2 160.2 %copy-start.3 = (s32[1,2,8192]{2,1,0:T(2,128)S(1)}, s32[1,2,8192]{2,1,0:T(2,128)}, u32[]{:S(2)}) copy-start(s32[1,2,8192]{2,1,0:T(2,128)} %param.13) | copy-start | bytes 196612
  7.2 160.2 %copy-start.2 = (s32[1,2,8192]{2,1,0:T(2,128)S(1)}, s32[1,2,8192]{2,1,0:T(2,128)}, u32[]{:S(2)}) copy-start(s32[1,2,8192]{2,1,0:T(2,128)} %param.14) | copy-start | bytes 196612
  7.2 285.5 %all-reduce.4.cloned.1.call-start = ((), (), s32[]{:S(2)}) async-start(), calls=%async_computation.1 | async-start | bytes 131072 | tf_op jit(solution)/shard_map/psum | solution.py:47
  8.0 284.7 %copy-start.4 = (f32[2,8192]{1,0:T(2,128)S(1)}, f32[2,8192]{1,0:T(2,128)}, u32[]{:S(2)}) copy-start(f32[2,8192]{1,0:T(2,128)} %param.12) | copy-start | bytes 196612
Sparse Core Ops, SparseCore 0:
  168.5 124.1 all-reduce.3
